TPU v7x, 32 devices: a whole 2x2x4 slice. The times are simulated.
32 devices in a mesh: map: 2 (over x), rows: 16 (over z, y, core).
Axes of the slice: x: 2, y: 2, z: 4, core: 2. Of those that a mesh axis runs over, the one named last changes fastest.
Arguments:
- density: bfloat16 [16, 2048, 2048], P('map', 'rows'), parts along dimension 0, may hold values from 0 to 2300, as said below
- lens_weight: float32 [8], replicated, may hold values from 0.05 to 0.5
- bin_distance: float32 [16], replicated, may hold values from 0.5 to 2.5, as said below
- plane_bin: int32 [8], replicated, may hold values from 0 to 15, as said below
- source_plane: int32 [1], replicated, may hold values from 1 to 7, as said below
Outputs:
- shear: float32 [2, 2, 2048, 2048], P('map', None, 'rows'), parts along dimension 0
There are 2 independent parts, one for each index of `map`. A program takes and returns all parts, laid end to end along the dimension named above; an argument that names none is the same for every part. Nothing has to cross between parts.
Inputs may be any that keep to these rules, and one draw needn't show every extreme that they name: `density`: positive. `bin_distance`: increasing. `plane_bin`: strictly increasing over the planes. `source_plane`: distinct and increasing.
All inputs are finite; a program needn't handle non-finite values.
Results may differ from a plain program's by a relative error of at most 0.0003.
Values sent between devices are 32-bit elements; how exact they have to be, the bound alone decides.
A program may use at most 64 MiB of HBM per device.

v0:
```python
import functools

import jax
import jax.numpy as jnp
import ml_dtypes
import numpy as np
from jax import lax
from jax.experimental import pallas as pl
from jax.experimental.pallas import tpu as pltpu
from jax.sharding import PartitionSpec as P

RADIX = 16
GROUP = RADIX // 2
ROWS16 = 16
MESH = pl.DeviceIdType.MESH
F32 = jnp.float32
BF16 = jnp.bfloat16


def split_table(table):
    high = table.astype(ml_dtypes.bfloat16)
    low = (table - high.astype(np.float64)).astype(ml_dtypes.bfloat16)
    return np.stack([high, low], axis=1)


def column_tables(total_rows, total_cols):
    block = total_cols // RADIX
    half = block // 2
    inside = np.arange(block)
    forward = np.zeros((GROUP, 2 * block, 2 * block))
    inverse = np.zeros((GROUP, 2 * block, 2 * block))
    for j in range(GROUP):
        for c in range(2):
            k = c * half + np.arange(half)
            freq = GROUP * k if j == 0 else j + RADIX * k
            angle = 2 * np.pi * ((inside[:, None] * freq[None, :]) % total_cols) / total_cols
            cos, sin = np.cos(angle), np.sin(angle)
            real = slice(c * block, c * block + half)
            imag = slice(c * block + half, (c + 1) * block)
            if j == 0:
                even = (k % 2 == 0)[None, :]
                cos_both = np.concatenate([np.where(even, cos, 0.0), np.where(even, 0.0, cos)])
                sin_both = np.concatenate([np.where(even, sin, 0.0), np.where(even, 0.0, sin)])
                fwd_re, fwd_im = cos_both, -sin_both
                inv_re, inv_im = 2 * cos_both, -2 * sin_both
                if c == 0:
                    sign = np.concatenate([(-1.0) ** inside, np.zeros(block)])
                    fwd_im[:, 0] = sign
                    inv_re[:, 0] = cos_both[:, 0]
                    inv_im[:, 0] = sign
            else:
                fwd_re = np.concatenate([cos, sin])
                fwd_im = np.concatenate([-sin, cos])
                inv_re = np.concatenate([cos, sin])
                inv_im = np.concatenate([-sin, cos])
            forward[j][:, real] = fwd_re
            forward[j][:, imag] = fwd_im
            inverse[j][real, :] = inv_re.T
            inverse[j][imag, :] = inv_im.T
    return split_table(forward), split_table(inverse / (total_rows * total_cols))


def row_tables(total_rows):
    block = total_rows // RADIX
    inside = np.arange(block)
    forward, inverse = [], []
    for k1 in range(RADIX):
        freq = k1 + RADIX * inside
        angle = 2 * np.pi * ((freq[:, None] * inside[None, :]) % total_rows) / total_rows
        cos, sin = np.cos(angle), np.sin(angle)
        forward.append(np.concatenate([cos, -sin], axis=1))
        inverse.append(np.concatenate([cos.T, sin.T], axis=1))
    return split_table(np.stack(forward)), split_table(np.stack(inverse))


def scaled(number, value):
    return value if number == 1.0 else (-value if number == -1.0 else value * np.float32(number))


def plus_of(a, b):
    return b if a is None else (a if b is None else a + b)


def minus_of(a, b):
    return a if b is None else (-b if a is None else a - b)


def rotate(value, step, length, orient):
    re, im = value
    if step == 0:
        return value
    cos, sin = np.cos(2 * np.pi * step / length), orient * np.sin(2 * np.pi * step / length)
    if 4 * step == length:
        return (None if im is None else -sin * im, sin * re)
    if im is None:
        return (re * np.float32(cos), re * np.float32(sin))
    return (
        re * np.float32(cos) - im * np.float32(sin),
        re * np.float32(sin) + im * np.float32(cos),
    )


def real_forward(values):
    n = len(values)
    if n == 1:
        return [(values[0], None)]
    even, odd = real_forward(values[0::2]), real_forward(values[1::2])
    out = [None] * (n // 2 + 1)
    for k in range(n // 4 + 1):
        turned = rotate(odd[k], k, n, -1.0)
        out[k] = (plus_of(even[k][0], turned[0]), plus_of(even[k][1], turned[1]))
        other = minus_of(turned[1], even[k][1])
        out[n // 2 - k] = (minus_of(even[k][0], turned[0]), other)
        if 4 * k == n:
            out[k] = (even[k][0], minus_of(None, odd[k][0]))
    return out


def real_inverse(values):
    n = 2 * (len(values) - 1)
    if n == 2:
        a, b = values[0][0], values[1][0]
        return [a + b, a - b]
    even, odd = [], []
    for k in range(n // 4 + 1):
        a, b = values[k], values[n // 2 - k]
        if k == 0 or 4 * k == n:
            if k == 0:
                even.append((a[0] + b[0], None))
                odd.append((a[0] - b[0], None))
            else:
                even.append((2.0 * a[0], None))
                odd.append((-2.0 * a[1], None))
            continue
        even.append((a[0] + b[0], a[1] - b[1]))
        odd.append(rotate((a[0] - b[0], a[1] + b[1]), k, n, 1.0))
    out = [None] * n
    out[0::2] = real_inverse(even)
    out[1::2] = real_inverse(odd)
    return out


def times_i(value, sign):
    return pltpu.roll(value, value.shape[1] // 2, 1) * sign


def packed_dft(values, orient, sign):
    n = len(values)
    if n == 1:
        return values
    even, odd = packed_dft(values[0::2], orient, sign), packed_dft(values[1::2], orient, sign)
    out = [None] * n
    for k in range(n // 2):
        value = odd[k]
        if 4 * k == n:
            value = times_i(value, sign) * np.float32(orient)
        elif k:
            angle = 2 * np.pi * k / n
            value = value * np.float32(np.cos(angle)) + times_i(value, sign) * np.float32(
                orient * np.sin(angle)
            )
        out[k] = even[k] + value
        out[k + n // 2] = even[k] - value
    return out


def halves(value):
    high = value.astype(BF16)
    return high, (value - high.astype(F32)).astype(BF16)


def product(a, b):
    def dot(x, y):
        return jnp.dot(x, y, preferred_element_type=F32)

    return dot(a[0], b[0]) + dot(a[0], b[1]) + dot(a[1], b[0])


def frequency(positions, length):
    return jnp.where(positions < length // 2, positions, positions - length).astype(F32) / length


def kernel(
    n, density, weight, bins, plane_bin, source, col_fwd, col_inv, row_fwd, row_inv, out,
    dens, tab_cf, tab_ci, tab_rf, tab_ri, part, sums, parts, sbuf, xin, zbuf, zconj, wbuf, gbuf,
    rbuf, acc, load_sem, send_m, recv_m, send_f, recv_f, send_r, recv_r, own_sem,
):
    planes, rows, cols = density.shape
    total_rows = rows * n
    block = cols // RADIX
    half = block // 2
    xblock = total_rows // RADIX
    me = lax.axis_index("rows")
    group = me // GROUP
    mine = me % GROUP

    loads = [pltpu.make_async_copy(density.at[l], dens.at[l], load_sem.at[l]) for l in range(planes)]
    for at, (src, dst) in enumerate(
        [(col_fwd, tab_cf), (row_fwd, tab_rf), (row_inv, tab_ri), (col_inv, tab_ci)]
    ):
        loads.append(pltpu.make_async_copy(src, dst, load_sem.at[planes + at]))
    for load in loads:
        load.start()

    barrier = pltpu.get_barrier_semaphore()

    @pl.loop(1, n)
    def _(off):
        pl.semaphore_signal(
            barrier, inc=1, device_id={"rows": (me + off) % n}, device_id_type=MESH
        )

    for l in range(planes):
        loads[l].wait()

        def add_rows(i, total, l=l):
            at = pl.ds(pl.multiple_of(i * ROWS16, ROWS16), ROWS16)
            pieces = [dens[l, at, a * block:(a + 1) * block].astype(F32) for a in range(RADIX)]
            while len(pieces) > 1:
                pieces = [x + y for x, y in zip(pieces[0::2], pieces[1::2])]
            return total + pieces[0]

        total = lax.fori_loop(0, rows // ROWS16, add_rows, jnp.zeros((ROWS16, block), F32))
        part[l:l + 1, :] = jnp.sum(total, axis=0, keepdims=True)

    pl.semaphore_wait(barrier, n - 1)

    def sums_copy(dst, slot):
        return pltpu.make_async_remote_copy(
            src_ref=part, dst_ref=sums.at[slot], send_sem=send_m.at[dst], recv_sem=recv_m.at[slot],
            device_id={"rows": dst}, device_id_type=MESH,
        )

    @pl.loop(1, n)
    def _(off):
        sums_copy((me + off) % n, me).start()

    sums[me] = part[...]

    @pl.loop(1, n)
    def _(off):
        sums_copy((me + off) % n, (me + off) % n).wait_recv()

    cells = np.float32(total_rows * cols)
    whole = jnp.sum(jnp.sum(sums[...], axis=0), axis=1, keepdims=True)
    mean = jnp.broadcast_to(whole / cells, (planes, block))
    source_plane = source[0]
    source_distance = jnp.full((1, block), bins[plane_bin[source_plane]], F32)
    scales, offset = [], None
    for l in range(planes):
        distance = jnp.full((1, block), bins[plane_bin[l]], F32)
        lens = jnp.full((1, block), jnp.where(l <= source_plane, weight[l], np.float32(0.0)), F32)
        coefficient = lens * (1.0 - distance / source_distance)
        scales.append(coefficient / mean[l:l + 1, :])
        offset = coefficient if offset is None else offset + coefficient

    @pl.loop(0, rows // ROWS16)
    def _(i):
        at = pl.ds(pl.multiple_of(i * ROWS16, ROWS16), ROWS16)
        values = []
        for a in range(RADIX):
            value = None
            for l in range(planes):
                term = dens[l, at, a * block:(a + 1) * block].astype(F32) * scales[l]
                value = term if value is None else value + term
            values.append(value - offset)
        spectrum = real_forward(values)
        parts[0, at, :block] = spectrum[0][0]
        parts[0, at, block:] = spectrum[GROUP][0]
        for j in range(1, GROUP):
            parts[j, at, :block] = spectrum[j][0]
            parts[j, at, block:] = spectrum[j][1]

    loads[planes].wait()

    def forward_copy(c, dst, slot):
        return pltpu.make_async_remote_copy(
            src_ref=sbuf.at[c, dst % GROUP],
            dst_ref=xin.at[c, pl.ds(pl.multiple_of(slot * rows, rows), rows)],
            send_sem=send_f.at[c, dst], recv_sem=recv_f.at[c, slot],
            device_id={"rows": dst}, device_id_type=MESH,
        )

    def forward_own(c):
        return pltpu.make_async_copy(
            sbuf.at[c, mine], xin.at[c, pl.ds(pl.multiple_of(me * rows, rows), rows)],
            own_sem.at[c],
        )

    for c in range(2):
        lanes = slice(c * block, (c + 1) * block)

        @pl.loop(0, GROUP)
        def _(j, c=c, lanes=lanes):
            sbuf[c, j] = product(halves(parts[j]), (tab_cf[j, 0, :, lanes], tab_cf[j, 1, :, lanes]))

        forward_own(c).start()

        @pl.loop(1, n)
        def _(off, c=c):
            forward_copy(c, (me + off) % n, me).start()

    lane = lax.broadcasted_iota(jnp.int32, (1, block), 1)
    sign = jnp.where(lane < half, np.float32(-1.0), np.float32(1.0))
    loads[planes + 1].wait()
    loads[planes + 2].wait()
    loads[planes + 3].wait()

    def return_copy(c, dst, slot):
        return pltpu.make_async_remote_copy(
            src_ref=gbuf.at[c, :, pl.ds(pl.multiple_of(dst * rows, rows), rows)],
            dst_ref=rbuf.at[c, slot],
            send_sem=send_r.at[c, dst % GROUP], recv_sem=recv_r.at[c, slot],
            device_id={"rows": dst}, device_id_type=MESH,
        )

    def return_own(c):
        return pltpu.make_async_copy(
            gbuf.at[c, :, pl.ds(pl.multiple_of(me * rows, rows), rows)], rbuf.at[c, mine],
            own_sem.at[2 + c],
        )

    def peer(off):
        return group * GROUP + (mine + off) % GROUP

    for c in range(2):
        forward_own(c).wait()

        @pl.loop(1, n)
        def _(off, c=c):
            forward_copy(c, (me + off) % n, (me + off) % n).wait_recv()

        def first_pass(target, conjugate, c=c):
            @pl.loop(0, xblock // ROWS16)
            def _(i):
                at = pl.multiple_of(i * ROWS16, ROWS16)
                values = [xin[c, pl.ds(at + a * xblock, ROWS16), :] for a in range(RADIX)]
                if conjugate:
                    values = [-sign * value for value in values]
                for k1, value in enumerate(packed_dft(values, -1.0, sign)):
                    target[k1, pl.ds(at, ROWS16), :] = value

        first_pass(zbuf, False)
        if c == 0:
            first_pass(zconj, True)

        @pl.loop(0, RADIX)
        def _(k1, c=c):
            def transform(value):
                stacked = jnp.concatenate([value, times_i(value, sign)], axis=0)
                return product((tab_rf[k1, 0], tab_rf[k1, 1]), halves(stacked))

            spectrum = transform(zbuf[k1])
            turned = times_i(spectrum, sign)
            shape = (xblock, block)
            kx = k1 + RADIX * lax.broadcasted_iota(jnp.int32, shape, 0)
            q = lax.broadcasted_iota(jnp.int32, shape, 1) % half
            k2 = c * half + q
            ky = jnp.where(mine == 0, GROUP * k2, mine + RADIX * k2)
            fx, fy = frequency(kx, total_rows), frequency(ky, cols)
            squared = fx * fx + fy * fy
            recip = 1.0 / jnp.where(squared > 0, squared, np.float32(1.0))
            plus = (fx * fx - fy * fy) * recip
            cross = 2.0 * fx * fy * recip
            nyquist = kx == total_rows // 2
            zero = jnp.zeros(shape, F32)
            direct, across = plus, jnp.where(nyquist, cross, zero)
            second = jnp.where(nyquist, zero, cross) * spectrum
            if c == 0:
                mirrored = transform(zconj[k1])
                packed = jnp.logical_and(q == 0, mine == 0)
                recip_n = 1.0 / (fx * fx + np.float32(0.25))
                plus_n = (fx * fx - np.float32(0.25)) * recip_n
                cross_n = -fx * recip_n
                odd_n = jnp.where(nyquist, zero, cross_n)
                even_n = jnp.where(nyquist, cross_n, zero)
                mirror_direct = jnp.where(packed, 0.5 * (plus - plus_n), zero)
                mirror_across = jnp.where(packed, -0.5 * odd_n, zero)
                direct = jnp.where(packed, 0.5 * (plus + plus_n), direct)
                across = jnp.where(packed, 0.5 * odd_n, across)
                second = jnp.where(packed, 0.5 * even_n * (spectrum - mirrored), second)
                first = (
                    direct * spectrum + across * turned
                    + mirror_direct * mirrored + mirror_across * times_i(mirrored, sign)
                )
            else:
                first = direct * spectrum + across * turned
            both = jnp.concatenate(
                [
                    jnp.concatenate([first, times_i(first, sign)], axis=0),
                    jnp.concatenate([second, times_i(second, sign)], axis=0),
                ],
                axis=1,
            )
            wbuf[k1] = product((tab_ri[k1, 0], tab_ri[k1, 1]), halves(both))

        @pl.loop(0, xblock // ROWS16)
        def _(i, c=c):
            at = pl.multiple_of(i * ROWS16, ROWS16)
            for f in range(2):
                values = [
                    wbuf[k1, pl.ds(at, ROWS16), f * block:(f + 1) * block] for k1 in range(RADIX)
                ]
                for a, value in enumerate(packed_dft(values, 1.0, sign)):
                    gbuf[c, f, pl.ds(at + a * xblock, ROWS16), :] = value

        return_own(c).start()

        @pl.loop(1, GROUP)
        def _(off, c=c):
            return_copy(c, peer(off), mine).start()

    for c in range(2):
        return_own(c).wait()

        @pl.loop(1, GROUP)
        def _(off, c=c):
            return_copy(c, peer(off), (mine + off) % GROUP).wait_recv()

        rows_of = slice(c * block, (c + 1) * block)

        @pl.loop(0, GROUP)
        def _(j, c=c, rows_of=rows_of):
            for f in range(2):
                value = product(
                    halves(rbuf[c, j, f]), (tab_ci[j, 0, rows_of, :], tab_ci[j, 1, rows_of, :])
                )
                acc[f, j] = value if c == 0 else acc[f, j] + value

    @pl.loop(0, rows // ROWS16)
    def _(i):
        at = pl.ds(pl.multiple_of(i * ROWS16, ROWS16), ROWS16)
        for f in range(2):
            values = [(acc[f, 0, at, :block], None)]
            values += [(acc[f, j, at, :block], acc[f, j, at, block:]) for j in range(1, GROUP)]
            values += [(acc[f, 0, at, block:], None)]
            for a, value in enumerate(real_inverse(values)):
                out[0, f, at, a * block:(a + 1) * block] = value

    @pl.loop(1, n)
    def _(off):
        sums_copy((me + off) % n, me).wait_send()
        for c in range(2):
            forward_copy(c, (me + off) % n, me).wait_send()

    @pl.loop(1, GROUP)
    def _(off):
        for c in range(2):
            return_copy(c, peer(off), mine).wait_send()


def on_device(n, density, lens_weight, bin_distance, plane_bin, source_plane):
    planes, rows, cols = density.shape
    total_rows = rows * n
    block, xblock = cols // RADIX, total_rows // RADIX
    col_fwd, col_inv = column_tables(total_rows, cols)
    row_fwd, row_inv = row_tables(total_rows)
    tables = [jnp.asarray(t) for t in (col_fwd, row_fwd, row_inv, col_inv)]
    smem = pl.BlockSpec(memory_space=pltpu.SMEM)
    anywhere = pl.BlockSpec(memory_space=pl.ANY)
    dma = pltpu.SemaphoreType.DMA
    return pl.pallas_call(
        functools.partial(kernel, n),
        out_shape=jax.ShapeDtypeStruct((1, 2, rows, cols), F32),
        in_specs=[anywhere, smem, smem, smem, smem, anywhere, anywhere, anywhere, anywhere],
        out_specs=pl.BlockSpec(memory_space=pltpu.VMEM),
        scratch_shapes=[
            pltpu.VMEM((planes, rows, cols), BF16),
            pltpu.VMEM(col_fwd.shape, BF16),
            pltpu.VMEM(col_inv.shape, BF16),
            pltpu.VMEM(row_fwd.shape, BF16),
            pltpu.VMEM(row_inv.shape, BF16),
            pltpu.VMEM((planes, block), F32),
            pltpu.VMEM((n, planes, block), F32),
            pltpu.VMEM((GROUP, rows, 2 * block), F32),
            pltpu.VMEM((2, GROUP, rows, block), F32),
            pltpu.VMEM((2, total_rows, block), F32),
            pltpu.VMEM((RADIX, xblock, block), F32),
            pltpu.VMEM((RADIX, xblock, block), F32),
            pltpu.VMEM((RADIX, xblock, 2 * block), F32),
            pltpu.VMEM((2, 2, total_rows, block), F32),
            pltpu.VMEM((2, GROUP, 2, rows, block), F32),
            pltpu.VMEM((2, GROUP, rows, 2 * block), F32),
            dma((planes + 4,)),
            dma((n,)),
            dma((n,)),
            dma((2, n)),
            dma((2, n)),
            dma((2, GROUP)),
            dma((2, GROUP)),
            dma((4,)),
        ],
        compiler_params=pltpu.CompilerParams(
            collective_id=0, has_side_effects=True, vmem_limit_bytes=56 * 2**20
        ),
    )(density, lens_weight, bin_distance, plane_bin, source_plane, tables[0], tables[3], tables[1], tables[2])


def solution(mesh):
    return jax.shard_map(
        functools.partial(on_device, mesh.shape["rows"]),
        mesh=mesh,
        in_specs=(P("map", "rows", None), P(), P(), P(), P()),
        out_specs=P("map", None, "rows", None),
        check_vma=False,
    )
```

profile of v0, /device:TPU:5, one launch (start us, length us, event | category | flops | bytes accessed | tf_op | source)
XLA Modules:
  0.0 101.4 jit_solution(11048165861944234317)
XLA Ops:
  0.7 97.6 %shard_map.91 = f32[1,2,128,2048]{3,2,1,0:T(8,128)} custom-call(bf16[8,128,2048]{2,1,0:T(8,128)(2,1)} %density.1, f32[8]{0:T(128)} %weight.1, f32[16]{0:T(128)} %bins.1, s32[8]{0:T(128)} %plane_bin.1, s32[1]{0:T(128)S(6)} %copy.11.source, bf16[8,2,256,256]{3,2,1,0:T(8,128)(2,1)} %constant.8.clone.col_fwd, bf16[8,2,256,256]{3,2,1,0:T(8,128)(2,1)} %constant.11.clone.col_inv, ...), custom_call_target="tpu_custom_call" | custom-call | tf_op jit(solution)/shard_map/pallas_call | solution.py:462
  98.2 3.1 %copy.12 = f32[1,2,128,2048]{3,2,1,0:T(8,128)} copy(f32[1,2,128,2048]{3,2,1,0:T(8,128)} %shard_map.91) | data formatting | bytes 4194304
where the time goes:
time: 102 us; the launch traced here: 101 us
  Pallas kernels  97.6 us (96%)
  local copies, waits for them, and re-layouts  3.14 us (3%)
    pallas_call x1, Pallas kernels, on_device(): pl.pallas_call(functools.partial(kernel, n), out_shape=jax.ShapeDtypeStru...  97.6 us
    unnamed x1, local copies, waits for them, and re-layouts  3.14 us

commit v1 on v0

--- a/solution.py
+++ b/solution.py
@@ -11,6 +11,7 @@
 
 RADIX = 16
 GROUP = RADIX // 2
+EARLY, MIDDLE = 7, 8
 ROWS16 = 16
 MESH = pl.DeviceIdType.MESH
 F32 = jnp.float32
@@ -199,7 +200,7 @@
         [(col_fwd, tab_cf), (row_fwd, tab_rf), (row_inv, tab_ri), (col_inv, tab_ci)]
     ):
         loads.append(pltpu.make_async_copy(src, dst, load_sem.at[planes + at]))
-    for load in loads:
+    for load in loads[:planes]:
         load.start()
 
     barrier = pltpu.get_barrier_semaphore()
@@ -222,6 +223,9 @@
 
         total = lax.fori_loop(0, rows // ROWS16, add_rows, jnp.zeros((ROWS16, block), F32))
         part[l:l + 1, :] = jnp.sum(total, axis=0, keepdims=True)
+
+    for load in loads[planes:]:
+        load.start()
 
     pl.semaphore_wait(barrier, n - 1)
 
@@ -287,18 +291,40 @@
             own_sem.at[c],
         )
 
+    def peer(off):
+        return group * GROUP + (mine + off) % GROUP
+
+    def send_across(c, i):
+        for far in range(1, n // GROUP):
+            dst = (group + far) % (n // GROUP) * GROUP + (mine + i) % GROUP
+            forward_copy(c, dst, me).start()
+
+    early, middle = EARLY, MIDDLE
+
     for c in range(2):
         lanes = slice(c * block, (c + 1) * block)
 
-        @pl.loop(0, GROUP)
+        @pl.loop(0, GROUP, unroll=4)
         def _(j, c=c, lanes=lanes):
             sbuf[c, j] = product(halves(parts[j]), (tab_cf[j, 0, :, lanes], tab_cf[j, 1, :, lanes]))
 
         forward_own(c).start()
-
-        @pl.loop(1, n)
-        def _(off, c=c):
-            forward_copy(c, (me + off) % n, me).start()
+        if c == 0:
+            @pl.loop(0, GROUP)
+            def _(i):
+                send_across(0, i)
+
+                @pl.when(i > 0)
+                def _():
+                    forward_copy(0, peer(i), me).start()
+        else:
+            @pl.loop(1, GROUP)
+            def _(i):
+                forward_copy(1, peer(i), me).start()
+
+                @pl.when(i <= early)
+                def _():
+                    send_across(1, i - 1)
 
     lane = lax.broadcasted_iota(jnp.int32, (1, block), 1)
     sign = jnp.where(lane < half, np.float32(-1.0), np.float32(1.0))
@@ -319,9 +345,6 @@
             gbuf.at[c, :, pl.ds(pl.multiple_of(me * rows, rows), rows)], rbuf.at[c, mine],
             own_sem.at[2 + c],
         )
-
-    def peer(off):
-        return group * GROUP + (mine + off) % GROUP
 
     for c in range(2):
         forward_own(c).wait()
@@ -344,7 +367,7 @@
         if c == 0:
             first_pass(zconj, True)
 
-        @pl.loop(0, RADIX)
+        @pl.loop(0, RADIX, unroll=4)
         def _(k1, c=c):
             def transform(value):
                 stacked = jnp.concatenate([value, times_i(value, sign)], axis=0)
@@ -394,6 +417,10 @@
             )
             wbuf[k1] = product((tab_ri[k1, 0], tab_ri[k1, 1]), halves(both))
 
+        if c == 0:
+            for i in range(early, middle):
+                send_across(1, i)
+
         @pl.loop(0, xblock // ROWS16)
         def _(i, c=c):
             at = pl.multiple_of(i * ROWS16, ROWS16)
@@ -409,6 +436,10 @@
         @pl.loop(1, GROUP)
         def _(off, c=c):
             return_copy(c, peer(off), mine).start()
+            if c == 0:
+                @pl.when(off < GROUP - middle + 1)
+                def _():
+                    send_across(1, middle + off - 1)
 
     for c in range(2):
         return_own(c).wait()
@@ -419,7 +450,7 @@
 
         rows_of = slice(c * block, (c + 1) * block)
 
-        @pl.loop(0, GROUP)
+        @pl.loop(0, GROUP, unroll=4)
         def _(j, c=c, rows_of=rows_of):
             for f in range(2):
                 value = product(
@@ -461,7 +492,7 @@
     dma = pltpu.SemaphoreType.DMA
     return pl.pallas_call(
         functools.partial(kernel, n),
-        out_shape=jax.ShapeDtypeStruct((1, 2, rows, cols), F32),
+        out_shape=pltpu.VMEM((1, 2, rows, cols), F32),
         in_specs=[anywhere, smem, smem, smem, smem, anywhere, anywhere, anywhere, anywhere],
         out_specs=pl.BlockSpec(memory_space=pltpu.VMEM),
         scratch_shapes=[

time: 102 us -> 86.9 us (0.85)
  Pallas kernels: 97.6 us -> 83.8 us
  local copies, waits for them, and re-layouts: 3.14 us -> 1.32 us
    pallas_call x1, Pallas kernels: 97.6 us -> 83.8 us  [on_device(): pl.pallas_call(functools.partial(kernel, n), out_shape=pltpu.VMEM((1, 2,...]
    unnamed x1, local copies, waits for them, and re-layouts: 3.14 us -> 1.32 us
where the time goes in v1:
time: 86.9 us; the launch traced here: 85.8 us
  Pallas kernels  83.8 us (96%)
  local copies, waits for them, and re-layouts  1.32 us (2%)
    pallas_call x1, Pallas kernels, on_device(): pl.pallas_call(functools.partial(kernel, n), out_shape=pltpu.VMEM((1, 2,...  83.8 us

profile of v1, /device:TPU:5, one launch (start us, length us, event | category | flops | bytes accessed | tf_op | source)
XLA Modules:
  0.0 85.8 jit_solution(8847104357853408971)
XLA Ops:
  0.7 83.8 %shard_map.91 = f32[1,2,128,2048]{3,2,1,0:T(8,128)S(1)} custom-call(bf16[8,128,2048]{2,1,0:T(8,128)(2,1)} %density.1, f32[8]{0:T(128)} %weight.1, f32[16]{0:T(128)} %bins.1, s32[8]{0:T(128)} %plane_bin.1, s32[1]{0:T(128)S(6)} %copy.12.source, bf16[8,2,256,256]{3,2,1,0:T(8,128)(2,1)} %constant.8.clone.col_fwd, ...), custom_call_target="tpu_custom_call" | custom-call | tf_op jit(solution)/shard_map/pallas_call | solution.py:493
  84.5 1.3 %copy.11 = f32[1,2,128,2048]{3,2,1,0:T(8,128)} copy(f32[1,2,128,2048]{3,2,1,0:T(8,128)S(1)} %shard_map.91) | data formatting | bytes 4194304

commit v2 on v1

--- a/solution.py
+++ b/solution.py
@@ -183,7 +183,7 @@
 
 def kernel(
     n, density, weight, bins, plane_bin, source, col_fwd, col_inv, row_fwd, row_inv, out,
-    dens, tab_cf, tab_ci, tab_rf, tab_ri, part, sums, parts, sbuf, xin, zbuf, zconj, wbuf, gbuf,
+    dens, tab_cf, tab_ci, tab_rf, tab_ri, part, sums, parts, sbuf, xin, zbuf, wbuf, gbuf,
     rbuf, acc, load_sem, send_m, recv_m, send_f, recv_f, send_r, recv_r, own_sem,
 ):
     planes, rows, cols = density.shape
@@ -332,18 +332,18 @@
     loads[planes + 2].wait()
     loads[planes + 3].wait()
 
-    def return_copy(c, dst, slot):
+    def return_copy(c, f, dst, slot):
         return pltpu.make_async_remote_copy(
-            src_ref=gbuf.at[c, :, pl.ds(pl.multiple_of(dst * rows, rows), rows)],
-            dst_ref=rbuf.at[c, slot],
-            send_sem=send_r.at[c, dst % GROUP], recv_sem=recv_r.at[c, slot],
+            src_ref=gbuf.at[c, f, pl.ds(pl.multiple_of(dst * rows, rows), rows)],
+            dst_ref=rbuf.at[c, slot, f],
+            send_sem=send_r.at[c, f, dst % GROUP], recv_sem=recv_r.at[c, f, slot],
             device_id={"rows": dst}, device_id_type=MESH,
         )
 
-    def return_own(c):
+    def return_own(c, f):
         return pltpu.make_async_copy(
-            gbuf.at[c, :, pl.ds(pl.multiple_of(me * rows, rows), rows)], rbuf.at[c, mine],
-            own_sem.at[2 + c],
+            gbuf.at[c, f, pl.ds(pl.multiple_of(me * rows, rows), rows)], rbuf.at[c, mine, f],
+            own_sem.at[2 + 2 * c + f],
         )
 
     for c in range(2):
@@ -353,21 +353,17 @@
         def _(off, c=c):
             forward_copy(c, (me + off) % n, (me + off) % n).wait_recv()
 
-        def first_pass(target, conjugate, c=c):
+        def first_pass(target, c=c):
             @pl.loop(0, xblock // ROWS16)
             def _(i):
                 at = pl.multiple_of(i * ROWS16, ROWS16)
                 values = [xin[c, pl.ds(at + a * xblock, ROWS16), :] for a in range(RADIX)]
-                if conjugate:
-                    values = [-sign * value for value in values]
                 for k1, value in enumerate(packed_dft(values, -1.0, sign)):
                     target[k1, pl.ds(at, ROWS16), :] = value
 
-        first_pass(zbuf, False)
-        if c == 0:
-            first_pass(zconj, True)
-
-        @pl.loop(0, RADIX, unroll=4)
+        first_pass(zbuf)
+
+        @pl.loop(0, RADIX, unroll=8)
         def _(k1, c=c):
             def transform(value):
                 stacked = jnp.concatenate([value, times_i(value, sign)], axis=0)
@@ -390,7 +386,7 @@
             direct, across = plus, jnp.where(nyquist, cross, zero)
             second = jnp.where(nyquist, zero, cross) * spectrum
             if c == 0:
-                mirrored = transform(zconj[k1])
+                mirrored = transform(-sign * zbuf[(RADIX - k1) % RADIX])
                 packed = jnp.logical_and(q == 0, mine == 0)
                 recip_n = 1.0 / (fx * fx + np.float32(0.25))
                 plus_n = (fx * fx - np.float32(0.25)) * recip_n
@@ -421,38 +417,37 @@
             for i in range(early, middle):
                 send_across(1, i)
 
-        @pl.loop(0, xblock // ROWS16)
-        def _(i, c=c):
-            at = pl.multiple_of(i * ROWS16, ROWS16)
-            for f in range(2):
+        for f in range(2):
+            @pl.loop(0, xblock // ROWS16)
+            def _(i, c=c, f=f):
+                at = pl.multiple_of(i * ROWS16, ROWS16)
                 values = [
                     wbuf[k1, pl.ds(at, ROWS16), f * block:(f + 1) * block] for k1 in range(RADIX)
                 ]
                 for a, value in enumerate(packed_dft(values, 1.0, sign)):
                     gbuf[c, f, pl.ds(at + a * xblock, ROWS16), :] = value
 
-        return_own(c).start()
-
-        @pl.loop(1, GROUP)
-        def _(off, c=c):
-            return_copy(c, peer(off), mine).start()
-            if c == 0:
-                @pl.when(off < GROUP - middle + 1)
-                def _():
-                    send_across(1, middle + off - 1)
+            return_own(c, f).start()
+
+            @pl.loop(1, GROUP)
+            def _(off, c=c, f=f):
+                return_copy(c, f, peer(off), mine).start()
+                if c == 0 and f == 0:
+                    @pl.when(off < GROUP - middle + 1)
+                    def _():
+                        send_across(1, middle + off - 1)
 
     for c in range(2):
-        return_own(c).wait()
-
-        @pl.loop(1, GROUP)
-        def _(off, c=c):
-            return_copy(c, peer(off), (mine + off) % GROUP).wait_recv()
-
         rows_of = slice(c * block, (c + 1) * block)
-
-        @pl.loop(0, GROUP, unroll=4)
-        def _(j, c=c, rows_of=rows_of):
-            for f in range(2):
+        for f in range(2):
+            return_own(c, f).wait()
+
+            @pl.loop(1, GROUP)
+            def _(off, c=c, f=f):
+                return_copy(c, f, peer(off), (mine + off) % GROUP).wait_recv()
+
+            @pl.loop(0, GROUP, unroll=4)
+            def _(j, c=c, f=f, rows_of=rows_of):
                 value = product(
                     halves(rbuf[c, j, f]), (tab_ci[j, 0, rows_of, :], tab_ci[j, 1, rows_of, :])
                 )
@@ -477,7 +472,8 @@
     @pl.loop(1, GROUP)
     def _(off):
         for c in range(2):
-            return_copy(c, peer(off), mine).wait_send()
+            for f in range(2):
+                return_copy(c, f, peer(off), mine).wait_send()
 
 
 def on_device(n, density, lens_weight, bin_distance, plane_bin, source_plane):
@@ -507,7 +503,6 @@
             pltpu.VMEM((2, GROUP, rows, block), F32),
             pltpu.VMEM((2, total_rows, block), F32),
             pltpu.VMEM((RADIX, xblock, block), F32),
-            pltpu.VMEM((RADIX, xblock, block), F32),
             pltpu.VMEM((RADIX, xblock, 2 * block), F32),
             pltpu.VMEM((2, 2, total_rows, block), F32),
             pltpu.VMEM((2, GROUP, 2, rows, block), F32),
@@ -517,9 +512,9 @@
             dma((n,)),
             dma((2, n)),
             dma((2, n)),
-            dma((2, GROUP)),
-            dma((2, GROUP)),
-            dma((4,)),
+            dma((2, 2, GROUP)),
+            dma((2, 2, GROUP)),
+            dma((6,)),
         ],
         compiler_params=pltpu.CompilerParams(
             collective_id=0, has_side_effects=True, vmem_limit_bytes=56 * 2**20

time: 86.9 us -> 85 us (0.978); the launches traced: 85.8 us -> 84.9 us
  Pallas kernels: 83.8 us -> 82.9 us
    pallas_call x1, Pallas kernels: 83.8 us -> 82.9 us  [on_device(): pl.pallas_call(functools.partial(kernel, n), out_shape=pltpu.VMEM((1, 2,...]
where the time goes in v2:
time: 85 us; the launch traced here: 84.9 us
  Pallas kernels  82.9 us (98%)
  local copies, waits for them, and re-layouts  1.32 us (2%)
    pallas_call x1, Pallas kernels, on_device(): pl.pallas_call(functools.partial(kernel, n), out_shape=pltpu.VMEM((1, 2,...  82.9 us

profile of v2, /device:TPU:5, one launch (start us, length us, event | category | flops | bytes accessed | tf_op | source)
XLA Modules:
  0.0 84.9 jit_solution(18050124611867708802)
XLA Ops:
  0.7 82.9 %shard_map.91 = f32[1,2,128,2048]{3,2,1,0:T(8,128)S(1)} custom-call(bf16[8,128,2048]{2,1,0:T(8,128)(2,1)} %density.1, f32[8]{0:T(128)} %weight.1, f32[16]{0:T(128)} %bins.1, s32[8]{0:T(128)} %plane_bin.1, s32[1]{0:T(128)S(6)} %copy.12.source, bf16[8,2,256,256]{3,2,1,0:T(8,128)(2,1)} %constant.8.clone.col_fwd, ...), custom_call_target="tpu_custom_call" | custom-call | tf_op jit(solution)/shard_map/pallas_call | solution.py:489
  83.5 1.3 %copy.11 = f32[1,2,128,2048]{3,2,1,0:T(8,128)} copy(f32[1,2,128,2048]{3,2,1,0:T(8,128)S(1)} %shard_map.91) | data formatting | bytes 4194304
